TPU v7x, 256 devices: a whole 4x4x8 slice. The times are simulated.
256 devices in a mesh: dp: 8 (over z_hi, x), row: 8 (over y, core), col: 4 (over z_lo).
Axes of the slice: x: 4, y: 4, z: 8 (z_hi: 2, z_lo: 4; z = z_hi * 4 + z_lo), core: 2. Of those that a mesh axis runs over, the one named last changes fastest.
Arguments:
- layer_input: bfloat16 [2048, 4096], P('dp', 'row'), may hold values from -200 to 200
- out_grad: bfloat16 [2048, 4096], P('dp', 'row'), may hold values from -6 to 6
- norm_gain: float32 [4096], P('row'), may hold values from 0.1 to 1.9
- up_weight: bfloat16 [4096, 16384], P('row', 'col'), may hold values from -0.09375 to 0.09375
- down_weight: bfloat16 [16384, 4096], P('col', 'row'), may hold values from -0.046875 to 0.046875
- up_accum: float32 [4096, 16384], P('row', ('col', 'dp')), may hold values from -1131.3708 to 1131.3708
- down_accum: float32 [16384, 4096], P(('col', 'dp'), 'row'), may hold values from -1131.3708 to 1131.3708
- up_rows: float32 [4096], P('row'), may hold values from 307.2 to 3072
- up_cols: float32 [16384], P(('col', 'dp')), may hold values from 307.2 to 3072
- down_rows: float32 [16384], P(('col', 'dp')), may hold values from 307.2 to 3072
- down_cols: float32 [4096], P('row'), may hold values from 307.2 to 3072
Outputs:
- input_grad: bfloat16 [2048, 4096], P('dp', 'row')
- up_update: bfloat16 [4096, 16384], P('row', ('col', 'dp'))
- down_update: bfloat16 [16384, 4096], P(('col', 'dp'), 'row')
- rows_up: float32 [4096], P('row')
- cols_up: float32 [16384], P(('col', 'dp'))
- rows_down: float32 [16384], P(('col', 'dp'))
- cols_down: float32 [4096], P('row')
All inputs are finite; a program needn't handle non-finite values.
Results may differ from a plain program's by a relative error of at most 0.013.
Values may be sent and summed in bfloat16 or wider, within the bound.
No kernel may reach another device: no remote copies, remote signals or barrier semaphores. Data moves between devices by JAX's collectives and lax.ppermute only.
A program may use at most 128 MiB of HBM per device.

v0:
```python
import jax
import jax.numpy as jnp
from jax import lax
from jax.sharding import PartitionSpec as P

D = 4096
FF = 16384


DECAY_RATE = 0.9
TINY_SQUARE = 1e-30
NORM_EPSILON = 1e-06
GELU_SCALE = 0.7978845608028654
GELU_CUBIC = 0.044715


def gelu_value(operand):
    tangent = jnp.tanh(GELU_SCALE * (operand + GELU_CUBIC * operand * operand * operand))
    return 0.5 * operand * (1.0 + tangent)


def gelu_slope(operand):
    tangent = jnp.tanh(GELU_SCALE * (operand + GELU_CUBIC * operand * operand * operand))
    return 0.5 * (1.0 + tangent) + 0.5 * operand * (1.0 - tangent * tangent) * GELU_SCALE * (
        1.0 + 3.0 * GELU_CUBIC * operand * operand
    )


def local(
    layer_input,
    out_grad,
    norm_gain,
    up_weight,
    down_weight,
    up_accum,
    down_accum,
    up_rows,
    up_cols,
    down_rows,
    down_cols,
):
    contract_first = (((0,), (0,)), ((), ()))
    contract_last = (((1,), (1,)), ((), ()))
    wide_input = layer_input.astype(jnp.float32)
    square_sum = lax.psum(jnp.sum(wide_input * wide_input, axis=1), "row")
    inverse = lax.rsqrt(square_sum[:, None] / D + NORM_EPSILON)
    normed = (wide_input * inverse * norm_gain).astype(jnp.bfloat16)
    pre_sum = lax.psum(
        jnp.dot(normed, up_weight, preferred_element_type=jnp.float32).astype(jnp.bfloat16), "row"
    )
    pre_act = lax.optimization_barrier(pre_sum)
    wide_pre = pre_act.astype(jnp.float32)
    activation = gelu_value(wide_pre).astype(jnp.bfloat16)
    slope = gelu_slope(wide_pre)
    act_grad = lax.psum(
        lax.dot_general(
            out_grad, down_weight, contract_last, preferred_element_type=jnp.float32
        ).astype(jnp.bfloat16),
        "row",
    ).astype(jnp.float32)
    hidden_grad = (act_grad * slope).astype(jnp.bfloat16)
    normed_grad = lax.psum(
        lax.dot_general(
            hidden_grad, up_weight, contract_last, preferred_element_type=jnp.float32
        ).astype(jnp.bfloat16),
        "col",
    ).astype(jnp.float32)
    gained = normed_grad * norm_gain
    projection = lax.psum(jnp.sum(gained * wide_input, axis=1), "row")
    input_grad = (
        out_grad.astype(jnp.float32)
        + inverse * gained
        - wide_input * inverse * inverse * inverse * projection[:, None] / D
    ).astype(jnp.bfloat16)
    columns = hidden_grad
    up_micro = (
        lax.psum_scatter(
            lax.dot_general(
                columns, normed, contract_first, preferred_element_type=jnp.float32
            ).astype(jnp.bfloat16),
            "dp",
            scatter_dimension=0,
            tiled=True,
        )
        .astype(jnp.float32)
        .T
    )
    columns = activation
    down_micro = lax.psum_scatter(
        lax.dot_general(
            columns, out_grad, contract_first, preferred_element_type=jnp.float32
        ).astype(jnp.bfloat16),
        "dp",
        scatter_dimension=0,
        tiled=True,
    ).astype(jnp.float32)
    up_total = up_accum + up_micro
    down_total = down_accum + down_micro
    up_square = up_total * up_total
    down_square = down_total * down_total
    up_colsum, down_rowsum = lax.psum(
        (jnp.sum(up_square, axis=0), jnp.sum(down_square, axis=1)), "row"
    )
    cols_up = DECAY_RATE * up_cols + (1.0 - DECAY_RATE) * (up_colsum / D + TINY_SQUARE)
    rows_down = DECAY_RATE * down_rows + (1.0 - DECAY_RATE) * (down_rowsum / D + TINY_SQUARE)
    up_rowsum, down_colsum = lax.psum(
        (jnp.sum(up_square, axis=1), jnp.sum(down_square, axis=0)), ("dp", "col")
    )
    rows_up = DECAY_RATE * up_rows + (1.0 - DECAY_RATE) * (up_rowsum / FF + TINY_SQUARE)
    cols_down = DECAY_RATE * down_cols + (1.0 - DECAY_RATE) * (down_colsum / FF + TINY_SQUARE)
    up_level = lax.psum(jnp.sum(rows_up), "row") / D
    down_level = lax.psum(jnp.sum(rows_down), ("dp", "col")) / FF
    up_update = (up_total * lax.rsqrt(rows_up[:, None] * cols_up[None, :] / up_level)).astype(
        jnp.bfloat16
    )
    down_update = (
        down_total * lax.rsqrt(rows_down[:, None] * cols_down[None, :] / down_level)
    ).astype(jnp.bfloat16)
    return (input_grad, up_update, down_update, rows_up, cols_up, rows_down, cols_down)


def solution(mesh):
    placed = (
        P("dp", "row"),
        P("dp", "row"),
        P("row"),
        P("row", "col"),
        P("col", "row"),
        P("row", ("col", "dp")),
        P(("col", "dp"), "row"),
        P("row"),
        P(("col", "dp")),
        P(("col", "dp")),
        P("row"),
    )
    return jax.shard_map(
        local,
        mesh=mesh,
        in_specs=placed,
        out_specs=(
            P("dp", "row"),
            P("row", ("col", "dp")),
            P(("col", "dp"), "row"),
            P("row"),
            P(("col", "dp")),
            P(("col", "dp")),
            P("row"),
        ),
        check_vma=False,
    )
```

profile of v0, /device:TPU:0, one launch (start us, length us, event | category | flops | bytes accessed | tf_op | source)
XLA Modules:
  0.0 521.8 jit_solution(15964494126947410258)
XLA Ops:
  7.2 0.0 all-reduce.8.cloned.1.call-start
  7.2 1.1 fusion.24
  8.3 13.1 %psum.77 = f32[256]{0:T(256)S(1)} all-reduce(f32[256]{0:T(256)S(1)} %fusion.24), channel_id=1, replica_groups=mesh['dp'=8,'row'=8,'col'=4] {'row'}, use_global_device_ids=true, to_apply=%region_1.0 | all-reduce | flops 256 | bytes 2048 | tf_op jit(solution)/shard_map/psum | solution.py:45
  21.5 5.1 convolution_convert_fusion.3
  26.5 2.6 convolution_convert_fusion.2
  29.2 0.0 all-reduce.8.cloned.1.call-update
  29.2 0.0 all-reduce.6.cloned.1.call-start
  29.2 78.2 %all-reduce.8.cloned.1.call-done = (bf16[256,4096]{1,0:T(8,128)(2,1)}, bf16[256,4096]{1,0:T(8,128)(2,1)}) async-done(((bf16[256,4096]{1,0:T(8,128)(2,1)}, bf16[256,4096]{1,0:T(8,128)(2,1)}), (bf16[256,4096]{1,0:T(8,128)(2,1)}, bf16[256,4096]{1,0:T(8,128)(2,1)})) %all-reduce.8.cloned.1.call-update) | async-done | bytes 4194320 | tf_op jit(solution)/shard_map/psum | solution.py:48
  107.4 4.6 fusion.6
  112.1 2.0 convolution_convert_fusion.4
  114.1 0.0 reduce-scatter.5.cloned.1.call-start
  114.2 5.8 %convolution_convert_fusion = bf16[4096,512]{1,0:T(8,128)(2,1)} fusion(bf16[256,512]{1,0:T(8,128)(2,1)S(1)} %copy-done.4, bf16[256,4096]{1,0:T(8,128)(2,1)} %get-tuple-element.24), kind=kOutput, calls=%fused_computation.7 | convolution fusion | flops 1086324736 | bytes 6553600 | tf_op jit(solution)/shard_map/dot_general | solution.py:90
  120.0 0.0 reduce-scatter.3.cloned.1.call-start
  120.1 3.3 convolution_convert_fusion.1
  123.4 0.0 reduce-scatter.3.cloned.1.call-update
  123.5 1.2 copy-done.3
  124.6 0.3 copy.18
  125.0 38.8 %all-reduce.6.cloned.1.call-done = bf16[256,512]{1,0:T(8,128)(2,1)} async-done(((bf16[256,512]{1,0:T(8,128)(2,1)}), bf16[256,512]{1,0:T(8,128)(2,1)}) %all-reduce.6.cloned.1.call-update) | async-done | bytes 262160 | tf_op jit(solution)/shard_map/psum | solution.py:62
  163.8 1.1 fusion.25
  164.9 128.9 %reduce-scatter.5.cloned.1.call-done = bf16[512,512]{1,0:T(8,128)(2,1)} async-done(((bf16[4096,512]{1,0:T(8,128)(2,1)}), bf16[512,512]{1,0:T(8,128)(2,1)}) %reduce-scatter.5.cloned.1.call-update) | async-done | bytes 524304 | tf_op jit(solution)/shard_map/reduce_scatter | solution.py:89
  293.9 1.4 multiply_reduce_fusion
  295.2 13.3 %psum.85 = f32[512]{0:T(512)S(1)} all-reduce(f32[512]{0:T(512)S(1)} %get-tuple-element.15), channel_id=1, replica_groups=mesh['dp'=8,'row'=8,'col'=4] {'row'}, use_global_device_ids=true, to_apply=%region_16.0 | all-reduce | flops 512 | bytes 4096 | tf_op jit(solution)/shard_map/psum | solution.py:101
  308.5 0.6 fusion.33
  309.1 111.8 %reduce-scatter.3.cloned.1.call-done = bf16[512,512]{1,0:T(8,128)(2,1)} async-done(((bf16[4096,512]{1,0:T(8,128)(2,1)}), bf16[512,512]{1,0:T(8,128)(2,1)}) %reduce-scatter.3.cloned.1.call-update) | async-done | bytes 524304 | tf_op jit(solution)/shard_map/reduce_scatter | solution.py:77
  421.0 1.3 multiply_reduce_fusion.2
  422.3 72.5 %all-reduce = (f32[512]{0:T(512)S(1)}, f32[]{:T(128)}, f32[512]{0:T(512)S(1)}) all-reduce(f32[512]{0:T(512)S(1)} %get-tuple-element.17, f32[]{:T(128)} %get-tuple-element.28, f32[512]{0:T(512)S(1)} %get-tuple-element.14), channel_id=1, replica_groups=mesh['dp'=8,'row'=8,'col'=4] {'dp','col'}, use_global_device_ids=true, to_apply=%region_9.0 | all-reduce | flops 1025 | bytes 8200 | tf_op jit(solution)/shard_map/psum | solution.py:106
  494.8 0.6 fusion.32
  495.4 13.0 %all-reduce.1 = (f32[256]{0:T(256)S(1)}, f32[]{:T(128)}, f32[512]{0:T(512)S(1)}) all-reduce(f32[256]{0:T(256)S(1)} %fusion.25, f32[]{:T(128)} %get-tuple-element.26, f32[512]{0:T(512)S(1)} %get-tuple-element.16), channel_id=1, replica_groups=mesh['dp'=8,'row'=8,'col'=4] {'row'}, use_global_device_ids=true, to_apply=%region_6.0 | all-reduce | flops 769 | bytes 6152 | tf_op jit(solution)/shard_map/psum | solution.py:69
  509.1 1.3 multiply_convert_fusion.1
  510.5 1.0 copy.19
  512.1 2.0 fusion.23
  514.1 1.1 multiply_convert_fusion
  (36 shorter events, 0.1 us)
Async XLA Ops:
  7.2 19.4 %copy-start.1 = (bf16[256,512]{1,0:T(8,128)(2,1)S(1)}, bf16[256,512]{1,0:T(8,128)(2,1)}, u32[]{:S(2)}) copy-start(bf16[256,512]{1,0:T(8,128)(2,1)} %param.11) | copy-start | bytes 786436
  7.2 19.4 %copy-start.5 = (f32[512]{0:T(512)S(1)}, f32[512]{0:T(512)}, u32[]{:S(2)}) copy-start(f32[512]{0:T(512)} %param.13) | copy-start | bytes 6148
  7.2 100.2 %all-reduce.8.cloned.1.call-start = ((), (), s32[]{:S(2)}) async-start(), calls=%async_computation.5 | async-start | bytes 8388608 | tf_op jit(solution)/shard_map/psum | solution.py:48
  21.5 5.1 copy-start.14
  29.2 134.6 %all-reduce.6.cloned.1.call-start = ((), (), s32[]{:S(2)}) async-start(), calls=%async_computation.2 | async-start | bytes 524288 | tf_op jit(solution)/shard_map/psum | solution.py:62
  107.4 4.6 copy-start.15
  112.1 2.1 copy-start.4
  114.1 179.8 %reduce-scatter.5.cloned.1.call-start = ((), (), s32[]{:S(2)}) async-start(), calls=%async_computation.4 | async-start | bytes 4718592 | tf_op jit(solution)/shard_map/reduce_scatter | solution.py:89
  120.0 300.9 %reduce-scatter.3.cloned.1.call-start = ((), (), s32[]{:S(2)}) async-start(), calls=%async_computation.3 | async-start | bytes 4718592 | tf_op jit(solution)/shard_map/reduce_scatter | solution.py:77
  123.4 1.2 copy-start.3
  123.4 170.4 %copy-start = (f32[512,512]{1,0:T(8,128)S(1)}, f32[512,512]{1,0:T(8,128)}, u32[]{:S(2)}) copy-start(f32[512,512]{1,0:T(8,128)} %param.17) | copy-start | bytes 3145732
  123.4 185.1 %copy-start.12 = (f32[512]{0:T(512)S(1)}, f32[512]{0:T(512)}, u32[]{:S(2)}) copy-start(f32[512]{0:T(512)} %param.20) | copy-start | bytes 6148
  123.4 371.4 %copy-start.13 = (f32[512]{0:T(512)S(1)}, f32[512]{0:T(512)}, u32[]{:S(2)}) copy-start(f32[512]{0:T(512)} %param.18) | copy-start | bytes 6148
  123.4 385.7 %copy-start.10 = (f32[512]{0:T(512)S(1)}, f32[512]{0:T(512)}, u32[]{:S(2)}) copy-start(f32[512]{0:T(512)} %param.19) | copy-start | bytes 6148
  124.6 387.5 %copy-start.11 = (f32[512]{0:T(512)S(1)}, f32[512]{0:T(512)}, u32[]{:S(2)}) copy-start(f32[512]{0:T(512)} %param.21) | copy-start | bytes 6148
  293.9 220.3 %copy-start.2 = (bf16[512,512]{1,0:T(8,128)(2,1)S(1)}, bf16[512,512]{1,0:T(8,128)(2,1)}, u32[]{:S(2)}) copy-start(bf16[512,512]{1,0:T(8,128)(2,1)} %reduce-scatter.5.cloned.1.call-done) | copy-start | bytes 1572868
  309.1 206.1 %copy-start.8 = (f32[512]{0:T(512)}, f32[512]{0:T(512)S(1)}, u32[]{:S(2)}) copy-start(f32[512]{0:T(512)S(1)} %get-tuple-element.29) | copy-start | bytes 6148
  495.4 19.8 %copy-start.9 = (f32[512]{0:T(512)}, f32[512]{0:T(512)S(1)}, u32[]{:S(2)}) copy-start(f32[512]{0:T(512)S(1)} %get-tuple-element.27) | copy-start | bytes 6148
  509.1 6.1 %copy-start.6 = (f32[512]{0:T(512)}, f32[512]{0:T(512)S(1)}, u32[]{:S(2)}) copy-start(f32[512]{0:T(512)S(1)} %multiply_add_fusion.2) | copy-start | bytes 6148
  512.1 3.1 copy-start.7
Sparse Core Ops, SparseCore 0:
  29.3 78.0 all-reduce.7
  114.2 49.5 all-reduce.5
  168.5 125.2 reduce-scatter.4
  298.5 122.4 reduce-scatter.2
where the time goes:
time: 525 us; the launch traced here: 522 us
  waiting for transfers between devices  358 us (68%)
  blocking collectives  112 us (21%)
  matrix products  18.8 us (4%)
  between operations  15.2 us (3%)
  other arithmetic  15.1 us (3%)
    reduce_scatter x1, waiting for transfers between devices, local(): lax.psum_scatter(lax.dot_general(columns, out_grad, contract_first, prefe...  129 us
    reduce_scatter x1, waiting for transfers between devices, local(): lax.psum_scatter(lax.dot_general(columns, normed, contract_first, preferr...  112 us
    psum x1, waiting for transfers between devices, local(): lax.psum(jnp.dot(normed, up_weight, preferred_element_type=jnp.float32).a...  78.2 us
    psum x1, blocking collectives, local(): lax.psum((jnp.sum(up_square, axis=1), jnp.sum(down_square, axis=0)), ('dp...  72.5 us
    psum x1, waiting for transfers between devices, local(): lax.psum(lax.dot_general(hidden_grad, up_weight, contract_last, preferred...  38.8 us
    psum x1, blocking collectives, local(): lax.psum((jnp.sum(up_square, axis=0), jnp.sum(down_square, axis=1)), 'row')  13.3 us
    psum x1, blocking collectives, local(): square_sum = lax.psum(jnp.sum(wide_input * wide_input, axis=1), 'row')  13.1 us
    psum x1, blocking collectives, local(): projection = lax.psum(jnp.sum(gained * wide_input, axis=1), 'row')  13 us
  transfers between devices with their start and end apart: 4, of which 4 were waited for; matrix products, arithmetic and copies ran while one was open for 2% of the time, Pallas kernels for 0%

commit v1 on v0

v1 whole, which is shorter than its diff:
```python
import functools

import jax
import jax.numpy as jnp
from jax import lax
from jax.experimental import pallas as pl
from jax.experimental.pallas import tpu as pltpu
from jax.sharding import Mesh
from jax.sharding import PartitionSpec as P

D = 4096
FF = 16384
N_DEVICES = 256

DECAY_RATE = 0.9
TINY_SQUARE = 1e-30
NORM_EPSILON = 1e-06
GELU_SCALE = 0.7978845608028654
GELU_CUBIC = 0.044715

TOK = 256
WIDTH = 512
HID = 4096
HALF = 2048
QUARTER = 64
BLOCK = 512
EXTRA = 128

BF = jnp.bfloat16
F32 = jnp.float32
LAST = (((1,), (1,)), ((), ()))
FIRST = (((0,), (0,)), ((), ()))


def split_parts(column):
    high = column.astype(BF).astype(F32)
    rest = column - high
    middle = rest.astype(BF).astype(F32)
    low = rest - middle
    lane = lax.broadcasted_iota(jnp.int32, (column.shape[0], EXTRA), 1)
    parts = jnp.where(lane == 0, high, jnp.where(lane == 1, middle, jnp.where(lane == 2, low, 0.0)))
    return parts.astype(BF)


def join_parts(block):
    return jnp.sum(block.astype(F32), axis=1, keepdims=True)


def as_column(row):
    return jnp.broadcast_to(row, (128, row.shape[1])).T[:, 0:1]


def whole(shape):
    return pl.BlockSpec(shape, lambda i, s: (0,) * len(shape))


def kernel_call(body, scalars, operands, outs, specs=None, scratch=(), name=None, flops=0):
    specs = specs or {}
    in_specs = [specs.get(i, whole(a.shape)) for i, a in enumerate(operands)]
    out_bytes = sum(s.size * s.dtype.itemsize for s in outs)
    return pl.pallas_call(
        body,
        out_shape=outs,
        grid_spec=pltpu.PrefetchScalarGridSpec(
            num_scalar_prefetch=1,
            grid=(1,),
            in_specs=in_specs,
            out_specs=[whole(s.shape) for s in outs],
            scratch_shapes=list(scratch),
        ),
        compiler_params=pltpu.CompilerParams(vmem_limit_bytes=48 * 1024 * 1024),
        cost_estimate=pl.CostEstimate(flops=flops, bytes_accessed=4 * out_bytes, transcendentals=0),
        name=name,
    )(scalars, *operands)


def shaped(*shape, dtype=BF):
    return jax.ShapeDtypeStruct(shape, dtype)


FORWARD_FLOPS = 2 * TOK * WIDTH * HALF


def pre_other_body(s, li, og, gain, w, lo, sums, out):
    wide = li[...].astype(F32)
    gained = (wide * gain[...]).astype(BF)
    lo[0:TOK, :] = gained
    lo[TOK:, :] = og[...]
    square = jnp.sum(wide * wide, axis=1, keepdims=True)
    sums[...] = jnp.broadcast_to(square, (TOK, 128))
    out[:, 0:HALF] = jnp.dot(gained, w[...], preferred_element_type=F32).astype(BF)
    out[:, HALF:] = split_parts(square)


def pre_own_body(s, lo, sums, w, received, p0, p1, p2, p3, total):
    total[:, 0:HALF] = (
        jnp.dot(lo[0:TOK, :], w[...], preferred_element_type=F32) + received[:, 0:HALF].astype(F32)
    ).astype(BF)
    total[:, HALF:] = split_parts(sums[:, 0:1] + join_parts(received[:, HALF:]))
    for k, piece in enumerate((p0, p1, p2, p3)):
        start = pl.multiple_of(lax.rem(s[1] + k, 4) * QUARTER, QUARTER)
        piece[...] = total[pl.ds(start, QUARTER), :]


def act_other_body(s, og, w, out):
    out[...] = lax.dot_general(og[...], w[...], LAST, preferred_element_type=F32).astype(BF)


def act_own_body(s, og, w, received, p0, p1, p2, p3, total):
    total[...] = (
        lax.dot_general(og[...], w[...], LAST, preferred_element_type=F32) + received[...].astype(F32)
    ).astype(BF)
    for k, piece in enumerate((p0, p1, p2, p3)):
        start = pl.multiple_of(lax.rem(s[1] + k, 4) * QUARTER, QUARTER)
        piece[...] = total[pl.ds(start, QUARTER), :]


def inverse_of(pieces):
    square = sum(join_parts(p[:, HALF:]) for p in pieces)
    return lax.rsqrt(square / D + NORM_EPSILON)


def activation_body(s, p0, p1, p2, p3, a0, a1, a2, a3, scratch):
    pieces = (p0, p1, p2, p3)
    inverse = inverse_of(pieces)
    pre = sum(p[:, 0:HALF].astype(F32) for p in pieces) * inverse
    pre = pre.astype(BF).astype(F32)
    tangent = jnp.tanh(GELU_SCALE * (pre + GELU_CUBIC * pre * pre * pre))
    scratch[...] = (0.5 * pre * (1.0 + tangent)).astype(BF)
    for k, out in enumerate((a0, a1, a2, a3)):
        start = pl.multiple_of(lax.rem(s[2] + k, 4) * BLOCK, BLOCK)
        out[...] = scratch[:, pl.ds(start, BLOCK)]


def hidden_body(s, p0, p1, p2, p3, q0, q1, q2, q3, h0, h1, h2, h3, own):
    pieces = (p0, p1, p2, p3)
    inverse = inverse_of(pieces)
    linear = sum(p[:, 0:HALF].astype(F32) for p in pieces)
    pre = (linear * inverse).astype(BF).astype(F32)
    tangent = jnp.tanh(GELU_SCALE * (pre + GELU_CUBIC * pre * pre * pre))
    slope = 0.5 * (1.0 + tangent) + 0.5 * pre * (1.0 - tangent * tangent) * GELU_SCALE * (
        1.0 + 3.0 * GELU_CUBIC * pre * pre
    )
    act_grad = sum(q[...].astype(F32) for q in (q0, q1, q2, q3))
    hidden = (act_grad * slope * inverse).astype(BF)
    own[:, 0:HALF] = hidden
    projection = jnp.sum(hidden.astype(F32) * linear, axis=1, keepdims=True)
    own[:, HALF:] = split_parts(projection * inverse * inverse / D)
    for k, out in enumerate((h0, h1, h2, h3)):
        start = pl.multiple_of(lax.rem(s[2] + k, 4) * BLOCK, BLOCK)
        out[...] = own[:, pl.ds(start, BLOCK)]


def normed_grad_body(s, mine, other, w, out, hidden):
    c, y = s[0], s[1]
    correction = jnp.zeros((TOK, 1), F32)
    for source, core in ((mine, c), (other, 1 - c)):
        column = pl.multiple_of(core * HALF, HALF)
        for k in range(4):
            row = pl.multiple_of(lax.rem(y - k + 4, 4) * QUARTER, QUARTER)
            block = source[k * QUARTER : (k + 1) * QUARTER, :]
            hidden[pl.ds(row, QUARTER), pl.ds(column, HALF)] = block[:, 0:HALF]
            own = join_parts(block[:, HALF:])
            hidden[pl.ds(row, QUARTER), pl.ds(pl.multiple_of(HID + core * EXTRA, EXTRA), EXTRA)] = split_parts(own)
    correction = join_parts(hidden[:, HID : HID + EXTRA]) + join_parts(hidden[:, HID + EXTRA :])
    out[:, 0:WIDTH] = lax.dot_general(hidden[:, 0:HID], w[...], LAST, preferred_element_type=F32).astype(BF)
    out[:, WIDTH:] = split_parts(correction)


def input_grad_body(s, n0, n1, n2, n3, li, og, gain, out):
    blocks = (n0, n1, n2, n3)
    normed_grad = sum(n[:, 0:WIDTH].astype(F32) for n in blocks)
    correction = sum(join_parts(n[:, WIDTH:]) for n in blocks)
    out[...] = (
        og[...].astype(F32) + gain[...] * normed_grad - li[...].astype(F32) * correction
    ).astype(BF)


def gather_body(s, *refs):
    sources, (inputs, grads) = refs[:8], refs[8:]
    x, h = s[2], s[3]
    for j, source in enumerate(sources):
        group = jnp.where(j < 4, h, 1 - h) * 4 + lax.rem(x - j % 4 + 4, 4)
        start = pl.multiple_of(group * TOK, TOK)
        inputs[pl.ds(start, TOK), :] = source[0:TOK, :]
        grads[pl.ds(start, TOK), :] = source[TOK:, :]


def place_pieces(s, sources, scratch):
    c, y, x = s[0], s[1], s[2]
    for j, source in enumerate(sources):
        h = c if j < 4 else 1 - c
        quarter = lax.rem(y - j % 4 + 4, 4)
        for k in range(4):
            group = h * 4 + lax.rem(x - k + 4, 4)
            start = pl.multiple_of((group * 4 + quarter) * QUARTER, QUARTER)
            scratch[pl.ds(start, QUARTER), :] = source[k * QUARTER : (k + 1) * QUARTER, :]


def down_total_body(s, *refs):
    sources, (grads, accum, total, stats), scratch = refs[:8], refs[8:12], refs[12]
    place_pieces(s, sources, scratch)
    value = accum[...] + lax.dot_general(scratch[...], grads[...], FIRST, preferred_element_type=F32)
    total[...] = value
    square = value * value
    columns = jnp.sum(square, axis=0, keepdims=True)
    stats[0:1, :] = jnp.sum(square.T, axis=0, keepdims=True)
    stats[1:2, :] = columns
    stats[2:3, :] = jnp.broadcast_to(jnp.sum(columns, axis=1, keepdims=True), (1, WIDTH))
    stats[3:, :] = jnp.zeros((5, WIDTH), F32)


def up_total_body(s, *refs):
    sources, (inputs, accum, down_stats, up_rows, down_rows, total, by_row, by_col), scratch = (
        refs[:8],
        refs[8:16],
        refs[16],
    )
    place_pieces(s, sources, scratch)
    value = accum[...] + lax.dot_general(inputs[...], scratch[...], FIRST, preferred_element_type=F32)
    total[...] = value
    square = value * value
    columns = jnp.sum(square, axis=0, keepdims=True)
    everything = jnp.sum(columns, axis=1, keepdims=True)
    up_prior = jnp.sum(up_rows[...], axis=1, keepdims=True)
    down_prior = jnp.sum(down_rows[...], axis=1, keepdims=True)
    up_level = DECAY_RATE * up_prior / 32 + (1.0 - DECAY_RATE) * (everything / FF)
    down_level = DECAY_RATE * down_prior / 8 + (1.0 - DECAY_RATE) * (down_stats[2:3, 0:1] / D)
    by_row[0:1, :] = columns
    by_row[1:2, :] = down_stats[0:1, :]
    by_row[2:3, :] = jnp.broadcast_to(up_level, (1, WIDTH))
    by_row[3:4, :] = jnp.broadcast_to(down_level, (1, WIDTH))
    by_row[4:, :] = jnp.zeros((4, WIDTH), F32)
    by_col[0:1, :] = jnp.sum(square.T, axis=0, keepdims=True)
    by_col[1:2, :] = down_stats[1:2, :]
    by_col[2:, :] = jnp.zeros((6, WIDTH), F32)


def update_body(s, up, down, by_row, by_col, ur, uc, dr, dc, up_out, down_out, ur_out, uc_out, dr_out, dc_out):
    def moment(prior, sums, count):
        return DECAY_RATE * prior + (1.0 - DECAY_RATE) * (sums / count + TINY_SQUARE)

    rows_up = moment(ur[...], by_col[0:1, :], FF)
    cols_up = moment(uc[...], by_row[0:1, :], D)
    rows_down = moment(dr[...], by_row[1:2, :], D)
    cols_down = moment(dc[...], by_col[1:2, :], FF)
    up_level = by_col[2:3, 0:1] / D + (1.0 - DECAY_RATE) * TINY_SQUARE
    down_level = by_col[3:4, 0:1] / FF + (1.0 - DECAY_RATE) * TINY_SQUARE
    ur_out[...], uc_out[...], dr_out[...], dc_out[...] = rows_up, cols_up, rows_down, cols_down
    up_out[...] = (up[...] * lax.rsqrt(as_column(rows_up) * cols_up / up_level)).astype(BF)
    down_out[...] = (down[...] * lax.rsqrt(as_column(rows_down) * cols_down / down_level)).astype(BF)


def shift(value, axis, step, size):
    return lax.ppermute(value, axis, [(i, (i + step) % size) for i in range(size)])


def to_owners(value, step):
    pairs = []
    for h in range(2):
        for x in range(4):
            for c in range(2):
                pairs.append((h * 8 + x * 2 + c, c * 8 + ((x + step) % 4) * 2 + h))
    return lax.ppermute(value, ("zh", "x", "c"), pairs)


def gather_pieces(pieces):
    block = jnp.concatenate([to_owners(p, k) for k, p in enumerate(pieces)], axis=0)
    mine = [block] + [shift(block, "y", k, 4) for k in (1, 2, 3)]
    return mine + [shift(b, "c", 1, 2) for b in mine]


def local(li, og, gain, wu, wd, au, ad, ur, uc, dr, dc):
    scalars = jnp.stack([lax.axis_index("c"), lax.axis_index("y"), lax.axis_index("x"), lax.axis_index("zh")]).astype(
        jnp.int32
    )
    row = lambda v: v.reshape(1, WIDTH)
    gain = row(gain)
    up_half = lambda f: pl.BlockSpec((WIDTH, HALF), lambda i, s: (0, f(s[0])))
    down_half = lambda f: pl.BlockSpec((HALF, WIDTH), lambda i, s: (f(s[0]), 0))
    other, mine = (lambda c: 1 - c), (lambda c: c)

    lo, sums, pre_sent = kernel_call(
        pre_other_body,
        scalars,
        (li, og, gain, wu),
        [shaped(2 * TOK, WIDTH), shaped(TOK, 128, dtype=F32), shaped(TOK, HALF + EXTRA)],
        specs={3: up_half(other)},
        name="pre_other",
        flops=FORWARD_FLOPS,
    )
    pre_received = shift(pre_sent, "c", 1, 2)
    (act_sent,) = kernel_call(
        act_other_body,
        scalars,
        (og, wd),
        [shaped(TOK, HALF)],
        specs={1: down_half(other)},
        name="act_other",
        flops=FORWARD_FLOPS,
    )
    act_received = shift(act_sent, "c", 1, 2)
    pre = kernel_call(
        pre_own_body,
        scalars,
        (lo, sums, wu, pre_received),
        [shaped(QUARTER, HALF + EXTRA)] * 4,
        specs={2: up_half(mine)},
        scratch=[pltpu.VMEM((TOK, HALF + EXTRA), BF)],
        name="pre_own",
        flops=FORWARD_FLOPS,
    )
    pre = [pre[0]] + [shift(pre[k], "y", k, 4) for k in (1, 2, 3)]
    act = kernel_call(
        act_own_body,
        scalars,
        (og, wd, act_received),
        [shaped(QUARTER, HALF)] * 4,
        specs={1: down_half(mine)},
        scratch=[pltpu.VMEM((TOK, HALF), BF)],
        name="act_own",
        flops=FORWARD_FLOPS,
    )
    act = [act[0]] + [shift(act[k], "y", k, 4) for k in (1, 2, 3)]

    lo_other = shift(lo, "zh", 1, 2)
    groups = [lo] + [shift(lo, "x", k, 4) for k in (1, 2, 3)]
    groups += [lo_other] + [shift(lo_other, "x", k, 4) for k in (1, 2, 3)]
    all_inputs, all_grads = kernel_call(
        gather_body, scalars, groups, [shaped(8 * TOK, WIDTH)] * 2, name="gather"
    )

    activation = kernel_call(
        activation_body,
        scalars,
        pre,
        [shaped(QUARTER, BLOCK)] * 4,
        scratch=[pltpu.VMEM((QUARTER, HALF), BF)],
        name="activation",
    )
    *hidden, own = kernel_call(
        hidden_body,
        scalars,
        (*pre, *act),
        [shaped(QUARTER, BLOCK)] * 4 + [shaped(QUARTER, HALF + EXTRA)],
        name="hidden",
    )
    activation = gather_pieces(activation)
    hidden = gather_pieces(hidden)

    own = jnp.concatenate([own] + [shift(own, "y", k, 4) for k in (1, 2, 3)], axis=0)
    own_other = shift(own, "c", 1, 2)
    (partial,) = kernel_call(
        normed_grad_body,
        scalars,
        (own, own_other, wu),
        [shaped(TOK, WIDTH + EXTRA)],
        scratch=[pltpu.VMEM((TOK, HID + 2 * EXTRA), BF)],
        name="normed_grad",
        flops=2 * FORWARD_FLOPS,
    )
    partials = [partial] + [shift(partial, "zl", k, 4) for k in (1, 2, 3)]
    (input_grad,) = kernel_call(
        input_grad_body, scalars, (*partials, li, og, gain), [shaped(TOK, WIDTH)], name="input_grad"
    )

    down_total, down_stats = kernel_call(
        down_total_body,
        scalars,
        (*activation, all_grads, ad),
        [shaped(BLOCK, WIDTH, dtype=F32), shaped(8, WIDTH, dtype=F32)],
        scratch=[pltpu.VMEM((8 * TOK, BLOCK), BF)],
        name="down_total",
        flops=2 * FORWARD_FLOPS,
    )
    up_total, by_row, by_col = kernel_call(
        up_total_body,
        scalars,
        (*hidden, all_inputs, au, down_stats, row(ur), row(dr)),
        [shaped(WIDTH, BLOCK, dtype=F32), shaped(8, WIDTH, dtype=F32), shaped(8, WIDTH, dtype=F32)],
        scratch=[pltpu.VMEM((8 * TOK, BLOCK), BF)],
        name="up_total",
        flops=2 * FORWARD_FLOPS,
    )
    by_row = lax.psum(by_row, ("y", "c"))
    level = (lax.broadcasted_iota(jnp.int32, by_row.shape, 0) & 6) == 2
    by_col = by_col + jnp.where(level, by_row, 0.0)
    for axis in ("x", "zl", "zh"):
        by_col = lax.psum(by_col, axis)
    up_update, down_update, *moments = kernel_call(
        update_body,
        scalars,
        (up_total, down_total, by_row, by_col, row(ur), row(uc), row(dr), row(dc)),
        [shaped(WIDTH, BLOCK), shaped(BLOCK, WIDTH)] + [shaped(1, WIDTH, dtype=F32)] * 4,
        name="update",
    )
    return (input_grad, up_update, down_update, *[m.reshape(WIDTH) for m in moments])


def solution(mesh):
    fine = Mesh(mesh.devices.reshape(2, 4, 4, 2, 4), ("zh", "x", "y", "c", "zl"))
    dp, row, col = ("zh", "x"), ("y", "c"), "zl"
    owner = ("zl", "zh", "x")
    placed = (
        P(dp, row),
        P(dp, row),
        P(row),
        P(row, col),
        P(col, row),
        P(row, owner),
        P(owner, row),
        P(row),
        P(owner),
        P(owner),
        P(row),
    )
    return jax.shard_map(
        local,
        mesh=fine,
        in_specs=placed,
        out_specs=(P(dp, row), P(row, owner), P(owner, row), P(row), P(owner), P(owner), P(row)),
        check_vma=False,
    )
```

time: 525 us -> 256 us (0.49)
  waiting for transfers between devices: 358 us -> 43.9 us
  starting transfers between devices: 0.16 us -> 95 us
  blocking collectives: 112 us -> 76 us
  Pallas kernels: 0 us -> 32.4 us
  matrix products: 18.8 us -> 0 us
  other arithmetic: 15.1 us -> 0.16 us
  between operations: 15.2 us -> 1.19 us
    reduce_scatter x2 -> x0, waiting for transfers between devices: 241 us -> none  [the longest x1 129 us: local(): lax.psum_scatter(lax.dot_general(columns, out_grad, contract_first, prefe...]
    psum x2 -> x0, waiting for transfers between devices: 117 us -> none  [the longest x1 78.2 us: local(): lax.psum(jnp.dot(normed, up_weight, preferred_element_type=jnp.float32).a...]
    ppermute x0 -> x44, starting transfers between devices: none -> 95 us  [the longest x36 84 us: shift(): lax.ppermute(value, axis, [(i, (i + step) % size) for i in range(size)])]
    ppermute x0 -> x44, waiting for transfers between devices: none -> 43.9 us  [the longest x36 24 us: shift(): lax.ppermute(value, axis, [(i, (i + step) % size) for i in range(size)])]
    psum x4, blocking collectives: 112 us -> 76 us  [the longest x3 50.4 us: local(): by_col = lax.psum(by_col, axis)]
    pallas_call x0 -> x12, Pallas kernels: none -> 32.4 us  [kernel_call(): pl.pallas_call(body, out_shape=outs, grid_spec=pltpu.PrefetchScalarGridSp...]
    dot_general x5 -> x0, matrix products: 18.8 us -> none  [the longest x1 5.85 us: local(): lax.dot_general(columns, out_grad, contract_first, preferred_element_type...]
    convert_element_type x4 -> x0, other arithmetic: 9 us -> none  [the longest x1 4.63 us: local(): hidden_grad = (act_grad * slope).astype(jnp.bfloat16)]
  transfers between devices with their start and end apart: 4 -> 44, of which waited for: 4 -> 11; matrix products, arithmetic and copies ran while one was open for 2% -> 0% of each run, Pallas kernels for 0% -> 11%
where the time goes in v1:
time: 256 us; the launch traced here: 251 us
  starting transfers between devices  95 us (37%)
  blocking collectives  76 us (30%)
  waiting for transfers between devices  43.9 us (17%)
  Pallas kernels  32.4 us (13%)
  local copies, waits for them, and re-layouts  2.77 us (1%)
    ppermute x36, starting transfers between devices, shift(): lax.ppermute(value, axis, [(i, (i + step) % size) for i in range(size)])  84 us
    psum x3, blocking collectives, local(): by_col = lax.psum(by_col, axis)  50.4 us
    pallas_call x12, Pallas kernels, kernel_call(): pl.pallas_call(body, out_shape=outs, grid_spec=pltpu.PrefetchScalarGridSp...  32.4 us
    psum x1, blocking collectives, local(): by_row = lax.psum(by_row, ('y', 'c'))  25.6 us
    ppermute x36, waiting for transfers between devices, shift(): lax.ppermute(value, axis, [(i, (i + step) % size) for i in range(size)])  24 us
    ppermute x8, waiting for transfers between devices, to_owners(): return lax.ppermute(value, ('zh', 'x', 'c'), pairs)  19.9 us
    ppermute x8, starting transfers between devices, to_owners(): return lax.ppermute(value, ('zh', 'x', 'c'), pairs)  11 us
  transfers between devices with their start and end apart: 44, of which 11 were waited for; matrix products, arithmetic and copies ran while one was open for 0% of the time, Pallas kernels for 11%

profile of v1, /device:TPU:0, one launch (start us, length us, event | category | flops | bytes accessed | tf_op | source)
XLA Modules:
  0.0 251.4 jit_solution(5822824845836366680)
XLA Ops:
  3.3 3.1 %pre_other.1 = (bf16[512,512]{1,0:T(8,128)(2,1)S(1)}, f32[256,128]{1,0:T(8,128)S(1)}, bf16[256,2176]{1,0:T(8,128)(2,1)S(1)}) custom-call(s32[4]{0:T(128)S(1)} %pad_add_fusion.s, bf16[256,512]{1,0:T(8,128)(2,1)S(1)} %copy-done.5, bf16[256,512]{1,0:T(8,128)(2,1)S(1)} %copy-done.1, f32[1,512]{1,0:T(1,128)S(1)} %bitcast.17, bf16[512,4096]{1,0:T(8,128)(2,1)} %w.9), custom_call_target="tpu_custom_call" | custom-call | flops 536870912 | bytes 7077888 | tf_op jit(solution)/shard_map/pre_other/pallas_call | solution.py:61
  9.3 3.0 %pre_own.1 = (bf16[64,2176]{1,0:T(8,128)(2,1)S(1)}, bf16[64,2176]{1,0:T(8,128)(2,1)S(1)}, bf16[64,2176]{1,0:T(8,128)(2,1)S(1)}, bf16[64,2176]{1,0:T(8,128)(2,1)S(1)}) custom-call(s32[4]{0:T(128)S(1)} %pad_add_fusion.s, bf16[512,512]{1,0:T(8,128)(2,1)S(1)} %get-tuple-element.40.lo.refs_0_, f32[256,128]{1,0:T(8,128)S(1)} %get-tuple-element.41.sums, ...), custom_call_target="tpu_custom_call" | custom-call | flops 536870912 | bytes 4456448 | tf_op jit(solution)/shard_map/pre_own/pallas_call | solution.py:61
  12.5 2.7 %collective-permute-start.2 = (bf16[64,2176]{1,0:T(8,128)(2,1)S(1)}, bf16[64,2176]{1,0:T(8,128)(2,1)S(1)}, u32[]{:S(2)}, u32[]{:S(2)}) collective-permute-start(bf16[64,2176]{1,0:T(8,128)(2,1)S(1)} %get-tuple-element.45), channel_id=1, source_target_pairs={{0,16},{8,24},{16,0},{24,8},{1,17},{9,25},{17,1},{25,9},{2,18},{10... | collective-permute-start | bytes 835592 | tf_op jit(solution)/shard_map/ppermute | solution.py:255
  16.5 3.0 %act_own.1 = (bf16[64,2048]{1,0:T(8,128)(2,1)S(1)}, bf16[64,2048]{1,0:T(8,128)(2,1)S(1)}, bf16[64,2048]{1,0:T(8,128)(2,1)S(1)}, bf16[64,2048]{1,0:T(8,128)(2,1)S(1)}) custom-call(s32[4]{0:T(128)S(1)} %pad_add_fusion.s, bf16[256,512]{1,0:T(8,128)(2,1)S(1)} %copy-done.2, bf16[4096,512]{1,0:T(8,128)(2,1)} %w.8, ...), custom_call_target="tpu_custom_call" | custom-call | flops 536870912 | bytes 4194304 | tf_op jit(solution)/shard_map/act_own/pallas_call | solution.py:61
  21.8 7.0 %collective-permute-done.1.p1 = bf16[64,2176]{1,0:T(8,128)(2,1)S(1)} collective-permute-done((bf16[64,2176]{1,0:T(8,128)(2,1)S(1)}, bf16[64,2176]{1,0:T(8,128)(2,1)S(1)}, u32[]{:S(2)}, u32[]{:S(2)}) %collective-permute-start.1) | collective-permute-done | bytes 278560 | tf_op jit(solution)/shard_map/ppermute | solution.py:255
  28.7 7.1 %collective-permute-start.29 = (bf16[512,512]{1,0:T(8,128)(2,1)S(1)}, bf16[512,512]{1,0:T(8,128)(2,1)S(1)}, u32[]{:S(2)}, u32[]{:S(2)}) collective-permute-start(bf16[512,512]{1,0:T(8,128)(2,1)S(1)} %get-tuple-element.40.lo.refs_0_), channel_id=1, source_target_pairs={{0,128},{128,0},{1,129},{129,1},{2,130},{130,2},{3,131},{131,3},{4... | collective-permute-start | bytes 1572872 | tf_op jit(solution)/shard_map/ppermute | solution.py:255
  35.9 2.8 %collective-permute-start.28 = (bf16[512,512]{1,0:T(8,128)(2,1)S(1)}, bf16[512,512]{1,0:T(8,128)(2,1)S(1)}, u32[]{:S(2)}, u32[]{:S(2)}) collective-permute-start(bf16[512,512]{1,0:T(8,128)(2,1)S(1)} %get-tuple-element.40.lo.refs_0_), channel_id=1, source_target_pairs={{0,96},{32,0},{64,32},{96,64},{1,97},{33,1},{65,33},{97,65},{2,98}... | collective-permute-start | bytes 1572872 | tf_op jit(solution)/shard_map/ppermute | solution.py:255
  44.8 8.9 %collective-permute-done.16 = bf16[64,512]{1,0:T(8,128)(2,1)S(1)} collective-permute-done((bf16[64,512]{1,0:T(8,128)(2,1)S(1)}, bf16[64,512]{1,0:T(8,128)(2,1)S(1)}, u32[]{:S(2)}, u32[]{:S(2)}) %collective-permute-start.16) | collective-permute-done | bytes 65568 | tf_op jit(solution)/shard_map/ppermute | solution.py:264
  55.2 4.2 %collective-permute-done.17 = bf16[64,512]{1,0:T(8,128)(2,1)S(1)} collective-permute-done((bf16[64,512]{1,0:T(8,128)(2,1)S(1)}, bf16[64,512]{1,0:T(8,128)(2,1)S(1)}, u32[]{:S(2)}, u32[]{:S(2)}) %collective-permute-start.17) | collective-permute-done | bytes 65568 | tf_op jit(solution)/shard_map/ppermute | solution.py:264
  59.4 3.2 %collective-permute-start.32 = (bf16[512,512]{1,0:T(8,128)(2,1)S(1)}, bf16[512,512]{1,0:T(8,128)(2,1)S(1)}, u32[]{:S(2)}, u32[]{:S(2)}) collective-permute-start(bf16[512,512]{1,0:T(8,128)(2,1)S(1)} %collective-permute-done.29.refs_4_), channel_id=1, source_target_pairs={{0,96},{32,0},{64,32},{96,64},{1,97},{33,1},{65,33},{97,65},{2,98}... | collective-permute-start | bytes 1572872 | tf_op jit(solution)/shard_map/ppermute | solution.py:255
  63.4 7.4 %collective-permute-done.9 = bf16[64,2176]{1,0:T(8,128)(2,1)S(1)} collective-permute-done((bf16[64,2176]{1,0:T(8,128)(2,1)S(1)}, bf16[64,2176]{1,0:T(8,128)(2,1)S(1)}, u32[]{:S(2)}, u32[]{:S(2)}) %collective-permute-start.9) | collective-permute-done | bytes 278560 | tf_op jit(solution)/shard_map/ppermute | solution.py:255
  70.8 1.8 collective-permute-start.31
  72.6 3.2 %collective-permute-start.18 = (bf16[64,512]{1,0:T(8,128)(2,1)S(1)}, bf16[64,512]{1,0:T(8,128)(2,1)S(1)}, u32[]{:S(2)}, u32[]{:S(2)}) collective-permute-start(bf16[64,512]{1,0:T(8,128)(2,1)S(1)} %get-tuple-element.55), channel_id=1, source_target_pairs={{0,96},{4,224},{32,0},{36,128},{64,32},{68,160},{96,64},{100,192},... | collective-permute-start | bytes 196616 | tf_op jit(solution)/shard_map/ppermute | solution.py:264
  77.4 1.8 collective-permute-start.35
  79.7 2.7 %collective-permute-start.36 = (bf16[64,512]{1,0:T(8,128)(2,1)S(1)}, bf16[64,512]{1,0:T(8,128)(2,1)S(1)}, u32[]{:S(2)}, u32[]{:S(2)}) collective-permute-start(bf16[64,512]{1,0:T(8,128)(2,1)S(1)} %get-tuple-element.60), channel_id=1, source_target_pairs={{0,96},{4,224},{32,0},{36,128},{64,32},{68,160},{96,64},{100,192},... | collective-permute-start | bytes 196616 | tf_op jit(solution)/shard_map/ppermute | solution.py:264
  82.3 6.3 %collective-permute-done.34 = bf16[64,512]{1,0:T(8,128)(2,1)S(1)} collective-permute-done((bf16[64,512]{1,0:T(8,128)(2,1)S(1)}, bf16[64,512]{1,0:T(8,128)(2,1)S(1)}, u32[]{:S(2)}, u32[]{:S(2)}) %collective-permute-start.34) | collective-permute-done | bytes 65568 | tf_op jit(solution)/shard_map/ppermute | solution.py:264
  88.6 29.1 %collective-permute-start.11 = (bf16[256,2176]{1,0:T(8,128)(2,1)S(1)}, bf16[256,2176]{1,0:T(8,128)(2,1)S(1)}, u32[]{:S(2)}, u32[]{:S(2)}) collective-permute-start(bf16[256,2176]{1,0:T(8,128)(2,1)S(1)} %constant_dynamic-update-slice_fusion.mine), channel_id=1, source_target_pairs={{0,4},{4,0},{1,5},{5,1},{2,6},{6,2},{3,7},{7,3},{8,12},{12,8},{9,1... | collective-permute-start | bytes 3342344 | tf_op jit(solution)/shard_map/ppermute | solution.py:255
  119.1 2.2 collective-permute-start.20
  121.5 3.2 %collective-permute-start.39 = (bf16[256,512]{1,0:T(8,128)(2,1)S(1)}, bf16[256,512]{1,0:T(8,128)(2,1)S(1)}, u32[]{:S(2)}, u32[]{:S(2)}) collective-permute-start(bf16[256,512]{1,0:T(8,128)(2,1)S(1)} %constant_dynamic-update-slice_fusion.8.refs_0_), channel_id=1, source_target_pairs={{0,24},{8,0},{16,8},{24,16},{1,25},{9,1},{17,9},{25,17},{2,26},{10... | collective-permute-start | bytes 786440 | tf_op jit(solution)/shard_map/ppermute | solution.py:255
  124.7 7.5 %collective-permute-start.38 = (bf16[256,512]{1,0:T(8,128)(2,1)S(1)}, bf16[256,512]{1,0:T(8,128)(2,1)S(1)}, u32[]{:S(2)}, u32[]{:S(2)}) collective-permute-start(bf16[256,512]{1,0:T(8,128)(2,1)S(1)} %constant_dynamic-update-slice_fusion.8.refs_0_), channel_id=1, source_target_pairs={{0,16},{8,24},{16,0},{24,8},{1,17},{9,25},{17,1},{25,9},{2,18},{10... | collective-permute-start | bytes 786440 | tf_op jit(solution)/shard_map/ppermute | solution.py:255
  132.2 9.9 %collective-permute-start.37 = (bf16[256,512]{1,0:T(8,128)(2,1)S(1)}, bf16[256,512]{1,0:T(8,128)(2,1)S(1)}, u32[]{:S(2)}, u32[]{:S(2)}) collective-permute-start(bf16[256,512]{1,0:T(8,128)(2,1)S(1)} %constant_dynamic-update-slice_fusion.8.refs_0_), channel_id=1, source_target_pairs={{0,8},{8,16},{16,24},{24,0},{1,9},{9,17},{17,25},{25,1},{2,10},{10... | collective-permute-start | bytes 786440 | tf_op jit(solution)/shard_map/ppermute | solution.py:255
  144.4 6.5 %collective-permute-done.37.refs_1_ = bf16[256,512]{1,0:T(8,128)(2,1)S(1)} collective-permute-done((bf16[256,512]{1,0:T(8,128)(2,1)S(1)}, bf16[256,512]{1,0:T(8,128)(2,1)S(1)}, u32[]{:S(2)}, u32[]{:S(2)}) %collective-permute-start.37) | collective-permute-done | bytes 262176 | tf_op jit(solution)/shard_map/ppermute | solution.py:255
  153.4 2.8 %gather.1 = (bf16[2048,512]{1,0:T(8,128)(2,1)}, bf16[2048,512]{1,0:T(8,128)(2,1)}) custom-call(s32[4]{0:T(128)S(1)} %pad_add_fusion.s, bf16[512,512]{1,0:T(8,128)(2,1)S(1)} %get-tuple-element.40.lo.refs_0_, bf16[512,512]{1,0:T(8,128)(2,1)S(1)} %collective-permute-done.26.refs_1_, bf16[512,512]{1,0:T(8,128)(2,1)S(1)} %collective-permute-done.27.refs_2_, ...), custom_call_target="tpu_custom_call" | custom-call | bytes 16777216 | tf_op jit(solution)/shard_map/gather/pallas_call | solution.py:61
  156.2 3.8 %down_total.1 = (f32[512,512]{1,0:T(8,128)S(1)}, f32[8,512]{1,0:T(8,128)S(1)}) custom-call(s32[4]{0:T(128)S(1)} %pad_add_fusion.s, bf16[256,512]{1,0:T(8,128)(2,1)S(1)} %constant_dynamic-update-slice_fusion.8.refs_0_, bf16[256,512]{1,0:T(8,128)(2,1)S(1)} %collective-permute-done.37.refs_1_, bf16[256,512]{1,0:T(8,128)(2,1)S(1)} %collective-permute-done.38.refs_2_, ...), custom_call_target="tpu_custom_call" | custom-call | flops 1073741824 | bytes 4259840 | tf_op jit(solution)/shard_map/down_total/pallas_call | solution.py:61
  160.0 4.3 %normed_grad.1.n0 = bf16[256,640]{1,0:T(8,128)(2,1)S(1)} custom-call(s32[4]{0:T(128)S(1)} %pad_add_fusion.s, bf16[256,2176]{1,0:T(8,128)(2,1)S(1)} %constant_dynamic-update-slice_fusion.mine, bf16[256,2176]{1,0:T(8,128)(2,1)S(1)} %collective-permute-done.11.other, bf16[512,4096]{1,0:T(8,128)(2,1)} %w.9), custom_call_target="tpu_custom_call" | custom-call | flops 1073741824 | bytes 1310720 | tf_op jit(solution)/shard_map/normed_grad/pallas_call | solution.py:61
  166.5 3.8 %up_total.1 = (f32[512,512]{1,0:T(8,128)S(1)}, f32[8,512]{1,0:T(8,128)S(1)}, f32[8,512]{1,0:T(8,128)S(1)}) custom-call(s32[4]{0:T(128)S(1)} %pad_add_fusion.s, bf16[256,512]{1,0:T(8,128)(2,1)S(1)} %constant_dynamic-update-slice_fusion.4.refs_0_, bf16[256,512]{1,0:T(8,128)(2,1)S(1)} %collective-permute-done.19.refs_1_, ...), custom_call_target="tpu_custom_call" | custom-call | flops 1073741824 | bytes 4325376 | tf_op jit(solution)/shard_map/up_total/pallas_call | solution.py:61
  170.3 25.6 %psum.28.by_row = f32[8,512]{1,0:T(8,128)S(1)} all-reduce(f32[8,512]{1,0:T(8,128)S(1)} %get-tuple-element.65), channel_id=1, replica_groups=mesh['zh'=2,'x'=4,'y'=4,'c'=2,'zl'=4] {'y','c'}, use_global_device_ids=true, to_apply=%region_0.0 | all-reduce | flops 4096 | bytes 32768 | tf_op jit(solution)/shard_map/psum | solution.py:385
  196.0 15.8 %psum.29 = f32[8,512]{1,0:T(8,128)S(1)} all-reduce(f32[8,512]{1,0:T(8,128)S(1)} %select_add_fusion), channel_id=1, replica_groups=mesh['zh'=2,'x'=4,'y'=4,'c'=2,'zl'=4] {'x'}, use_global_device_ids=true, to_apply=%region_1.2 | all-reduce | flops 4096 | bytes 32768 | tf_op jit(solution)/shard_map/psum | solution.py:389
  211.8 17.2 %psum.30 = f32[8,512]{1,0:T(8,128)S(1)} all-reduce(f32[8,512]{1,0:T(8,128)S(1)} %psum.29), channel_id=1, replica_groups=mesh['zh'=2,'x'=4,'y'=4,'c'=2,'zl'=4] {'zl'}, use_global_device_ids=true, to_apply=%region_2.3 | all-reduce | flops 4096 | bytes 32768 | tf_op jit(solution)/shard_map/psum | solution.py:389
  229.0 17.4 %psum.31.by_col = f32[8,512]{1,0:T(8,128)S(1)} all-reduce(f32[8,512]{1,0:T(8,128)S(1)} %psum.30), channel_id=1, replica_groups=mesh['zh'=2,'x'=4,'y'=4,'c'=2,'zl'=4] {'zh'}, use_global_device_ids=true, to_apply=%region_3.4 | all-reduce | flops 4096 | bytes 32768 | tf_op jit(solution)/shard_map/psum | solution.py:389
  246.4 2.1 update.1
  248.5 2.7 %input_grad.1 = bf16[256,512]{1,0:T(8,128)(2,1)} custom-call(s32[4]{0:T(128)S(1)} %pad_add_fusion.s, bf16[256,640]{1,0:T(8,128)(2,1)S(1)} %normed_grad.1.n0, bf16[256,640]{1,0:T(8,128)(2,1)} %collective-permute-done.12.n1, bf16[256,640]{1,0:T(8,128)(2,1)} %collective-permute-done.13.n2, bf16[256,640]{1,0:T(8,128)(2,1)S(1)} %collective-permute-done.14.n3, ...), custom_call_target="tpu_custom_call" | custom-call | bytes 1048576 | tf_op jit(solution)/shard_map/input_grad/pallas_call | solution.py:61
  (113 shorter events, 28.1 us)
Async XLA Ops:
  12.4 16.4 %collective-permute-start.1 = (bf16[64,2176]{1,0:T(8,128)(2,1)S(1)}, bf16[64,2176]{1,0:T(8,128)(2,1)S(1)}, u32[]{:S(2)}, u32[]{:S(2)}) collective-permute-start(bf16[64,2176]{1,0:T(8,128)(2,1)S(1)} %get-tuple-element.44), channel_id=1, source_target_pairs={{0,8},{8,16},{16,24},{24,0},{1,9},{9,17},{17,25},{25,1},{2,10},{10... | collective-permute-start | bytes 835592 | tf_op jit(solution)/shard_map/ppermute | solution.py:255
  12.5 16.3 %collective-permute-start.2 = (bf16[64,2176]{1,0:T(8,128)(2,1)S(1)}, bf16[64,2176]{1,0:T(8,128)(2,1)S(1)}, u32[]{:S(2)}, u32[]{:S(2)}) collective-permute-start(bf16[64,2176]{1,0:T(8,128)(2,1)S(1)} %get-tuple-element.45), channel_id=1, source_target_pairs={{0,16},{8,24},{16,0},{24,8},{1,17},{9,25},{17,1},{25,9},{2,18},{10... | collective-permute-start | bytes 835592 | tf_op jit(solution)/shard_map/ppermute | solution.py:255
  15.2 20.7 %collective-permute-start.3 = (bf16[64,2176]{1,0:T(8,128)(2,1)S(1)}, bf16[64,2176]{1,0:T(8,128)(2,1)S(1)}, u32[]{:S(2)}, u32[]{:S(2)}) collective-permute-start(bf16[64,2176]{1,0:T(8,128)(2,1)S(1)} %get-tuple-element.46), channel_id=1, source_target_pairs={{0,24},{8,0},{16,8},{24,16},{1,25},{9,1},{17,9},{25,17},{2,26},{10... | collective-permute-start | bytes 835592 | tf_op jit(solution)/shard_map/ppermute | solution.py:255
  19.5 20.1 %collective-permute-start.5 = (bf16[64,2048]{1,0:T(8,128)(2,1)S(1)}, bf16[64,2048]{1,0:T(8,128)(2,1)S(1)}, u32[]{:S(2)}, u32[]{:S(2)}) collective-permute-start(bf16[64,2048]{1,0:T(8,128)(2,1)S(1)} %get-tuple-element.48), channel_id=1, source_target_pairs={{0,8},{8,16},{16,24},{24,0},{1,9},{9,17},{17,25},{25,1},{2,10},{10... | collective-permute-start | bytes 786440 | tf_op jit(solution)/shard_map/ppermute | solution.py:255
  20.3 20.2 %collective-permute-start.6 = (bf16[64,2048]{1,0:T(8,128)(2,1)S(1)}, bf16[64,2048]{1,0:T(8,128)(2,1)S(1)}, u32[]{:S(2)}, u32[]{:S(2)}) collective-permute-start(bf16[64,2048]{1,0:T(8,128)(2,1)S(1)} %get-tuple-element.49), channel_id=1, source_target_pairs={{0,16},{8,24},{16,0},{24,8},{1,17},{9,25},{17,1},{25,9},{2,18},{10... | collective-permute-start | bytes 786440 | tf_op jit(solution)/shard_map/ppermute | solution.py:255
  28.7 12.4 %collective-permute-start.7 = (bf16[64,2048]{1,0:T(8,128)(2,1)S(1)}, bf16[64,2048]{1,0:T(8,128)(2,1)S(1)}, u32[]{:S(2)}, u32[]{:S(2)}) collective-permute-start(bf16[64,2048]{1,0:T(8,128)(2,1)S(1)} %get-tuple-element.50), channel_id=1, source_target_pairs={{0,24},{8,0},{16,8},{24,16},{1,25},{9,1},{17,9},{25,17},{2,26},{10... | collective-permute-start | bytes 786440 | tf_op jit(solution)/shard_map/ppermute | solution.py:255
  28.7 25.7 %collective-permute-start.29 = (bf16[512,512]{1,0:T(8,128)(2,1)S(1)}, bf16[512,512]{1,0:T(8,128)(2,1)S(1)}, u32[]{:S(2)}, u32[]{:S(2)}) collective-permute-start(bf16[512,512]{1,0:T(8,128)(2,1)S(1)} %get-tuple-element.40.lo.refs_0_), channel_id=1, source_target_pairs={{0,128},{128,0},{1,129},{129,1},{2,130},{130,2},{3,131},{131,3},{4... | collective-permute-start | bytes 1572872 | tf_op jit(solution)/shard_map/ppermute | solution.py:255
  35.9 35.0 %collective-permute-start.28 = (bf16[512,512]{1,0:T(8,128)(2,1)S(1)}, bf16[512,512]{1,0:T(8,128)(2,1)S(1)}, u32[]{:S(2)}, u32[]{:S(2)}) collective-permute-start(bf16[512,512]{1,0:T(8,128)(2,1)S(1)} %get-tuple-element.40.lo.refs_0_), channel_id=1, source_target_pairs={{0,96},{32,0},{64,32},{96,64},{1,97},{33,1},{65,33},{97,65},{2,98}... | collective-permute-start | bytes 1572872 | tf_op jit(solution)/shard_map/ppermute | solution.py:255
  39.6 33.0 %collective-permute-start.27 = (bf16[512,512]{1,0:T(8,128)(2,1)S(1)}, bf16[512,512]{1,0:T(8,128)(2,1)S(1)}, u32[]{:S(2)}, u32[]{:S(2)}) collective-permute-start(bf16[512,512]{1,0:T(8,128)(2,1)S(1)} %get-tuple-element.40.lo.refs_0_), channel_id=1, source_target_pairs={{0,64},{32,96},{64,0},{96,32},{1,65},{33,97},{65,1},{97,33},{2,66}... | collective-permute-start | bytes 1572872 | tf_op jit(solution)/shard_map/ppermute | solution.py:255
  42.7 20.0 %collective-permute-start.8 = (bf16[64,2176]{1,0:T(8,128)(2,1)S(1)}, bf16[64,2176]{1,0:T(8,128)(2,1)S(1)}, u32[]{:S(2)}, u32[]{:S(2)}) collective-permute-start(bf16[64,2176]{1,0:T(8,128)(2,1)S(1)} %get-tuple-element.51), channel_id=1, source_target_pairs={{0,8},{8,16},{16,24},{24,0},{1,9},{9,17},{17,25},{25,1},{2,10},{10... | collective-permute-start | bytes 835592 | tf_op jit(solution)/shard_map/ppermute | solution.py:255
  43.5 10.1 %collective-permute-start.16 = (bf16[64,512]{1,0:T(8,128)(2,1)S(1)}, bf16[64,512]{1,0:T(8,128)(2,1)S(1)}, u32[]{:S(2)}, u32[]{:S(2)}) collective-permute-start(bf16[64,512]{1,0:T(8,128)(2,1)S(1)} %get-tuple-element.53), channel_id=1, source_target_pairs={{0,32},{4,160},{32,64},{36,192},{64,96},{68,224},{96,0},{100,128},... | collective-permute-start | bytes 196616 | tf_op jit(solution)/shard_map/ppermute | solution.py:264
  54.5 18.1 %collective-permute-start.26 = (bf16[512,512]{1,0:T(8,128)(2,1)S(1)}, bf16[512,512]{1,0:T(8,128)(2,1)S(1)}, u32[]{:S(2)}, u32[]{:S(2)}) collective-permute-start(bf16[512,512]{1,0:T(8,128)(2,1)S(1)} %get-tuple-element.40.lo.refs_0_), channel_id=1, source_target_pairs={{0,32},{32,64},{64,96},{96,0},{1,33},{33,65},{65,97},{97,1},{2,34}... | collective-permute-start | bytes 1572872 | tf_op jit(solution)/shard_map/ppermute | solution.py:255
  59.4 18.0 %collective-permute-start.32 = (bf16[512,512]{1,0:T(8,128)(2,1)S(1)}, bf16[512,512]{1,0:T(8,128)(2,1)S(1)}, u32[]{:S(2)}, u32[]{:S(2)}) collective-permute-start(bf16[512,512]{1,0:T(8,128)(2,1)S(1)} %collective-permute-done.29.refs_4_), channel_id=1, source_target_pairs={{0,96},{32,0},{64,32},{96,64},{1,97},{33,1},{65,33},{97,65},{2,98}... | collective-permute-start | bytes 1572872 | tf_op jit(solution)/shard_map/ppermute | solution.py:255
  70.8 50.5 %collective-permute-start.31 = (bf16[512,512]{1,0:T(8,128)(2,1)S(1)}, bf16[512,512]{1,0:T(8,128)(2,1)S(1)}, u32[]{:S(2)}, u32[]{:S(2)}) collective-permute-start(bf16[512,512]{1,0:T(8,128)(2,1)S(1)} %collective-permute-done.29.refs_4_), channel_id=1, source_target_pairs={{0,64},{32,96},{64,0},{96,32},{1,65},{33,97},{65,1},{97,33},{2,66}... | collective-permute-start | bytes 1572872 | tf_op jit(solution)/shard_map/ppermute | solution.py:255
  72.6 48.8 %collective-permute-start.30 = (bf16[512,512]{1,0:T(8,128)(2,1)S(1)}, bf16[512,512]{1,0:T(8,128)(2,1)S(1)}, u32[]{:S(2)}, u32[]{:S(2)}) collective-permute-start(bf16[512,512]{1,0:T(8,128)(2,1)S(1)} %collective-permute-done.29.refs_4_), channel_id=1, source_target_pairs={{0,32},{32,64},{64,96},{96,0},{1,33},{33,65},{65,97},{97,1},{2,34}... | collective-permute-start | bytes 1572872 | tf_op jit(solution)/shard_map/ppermute | solution.py:255
  77.3 11.3 %collective-permute-start.34 = (bf16[64,512]{1,0:T(8,128)(2,1)S(1)}, bf16[64,512]{1,0:T(8,128)(2,1)S(1)}, u32[]{:S(2)}, u32[]{:S(2)}) collective-permute-start(bf16[64,512]{1,0:T(8,128)(2,1)S(1)} %get-tuple-element.58), channel_id=1, source_target_pairs={{0,32},{4,160},{32,64},{36,192},{64,96},{68,224},{96,0},{100,128},... | collective-permute-start | bytes 196616 | tf_op jit(solution)/shard_map/ppermute | solution.py:264
  77.4 40.4 %collective-permute-start.35 = (bf16[64,512]{1,0:T(8,128)(2,1)S(1)}, bf16[64,512]{1,0:T(8,128)(2,1)S(1)}, u32[]{:S(2)}, u32[]{:S(2)}) collective-permute-start(bf16[64,512]{1,0:T(8,128)(2,1)S(1)} %get-tuple-element.59), channel_id=1, source_target_pairs={{0,64},{4,192},{32,96},{36,224},{64,0},{68,128},{96,32},{100,160},... | collective-permute-start | bytes 196616 | tf_op jit(solution)/shard_map/ppermute | solution.py:264
  79.7 39.4 %collective-permute-start.36 = (bf16[64,512]{1,0:T(8,128)(2,1)S(1)}, bf16[64,512]{1,0:T(8,128)(2,1)S(1)}, u32[]{:S(2)}, u32[]{:S(2)}) collective-permute-start(bf16[64,512]{1,0:T(8,128)(2,1)S(1)} %get-tuple-element.60), channel_id=1, source_target_pairs={{0,96},{4,224},{32,0},{36,128},{64,32},{68,160},{96,64},{100,192},... | collective-permute-start | bytes 196616 | tf_op jit(solution)/shard_map/ppermute | solution.py:264
  88.6 71.3 %collective-permute-start.11 = (bf16[256,2176]{1,0:T(8,128)(2,1)S(1)}, bf16[256,2176]{1,0:T(8,128)(2,1)S(1)}, u32[]{:S(2)}, u32[]{:S(2)}) collective-permute-start(bf16[256,2176]{1,0:T(8,128)(2,1)S(1)} %constant_dynamic-update-slice_fusion.mine), channel_id=1, source_target_pairs={{0,4},{4,0},{1,5},{5,1},{2,6},{6,2},{3,7},{7,3},{8,12},{12,8},{9,1... | collective-permute-start | bytes 3342344 | tf_op jit(solution)/shard_map/ppermute | solution.py:255
  119.1 13.1 %collective-permute-start.20 = (bf16[256,512]{1,0:T(8,128)(2,1)S(1)}, bf16[256,512]{1,0:T(8,128)(2,1)S(1)}, u32[]{:S(2)}, u32[]{:S(2)}) collective-permute-start(bf16[256,512]{1,0:T(8,128)(2,1)S(1)} %constant_dynamic-update-slice_fusion.4.refs_0_), channel_id=1, source_target_pairs={{0,16},{8,24},{16,0},{24,8},{1,17},{9,25},{17,1},{25,9},{2,18},{10... | collective-permute-start | bytes 786440 | tf_op jit(solution)/shard_map/ppermute | solution.py:255
  121.4 20.8 %collective-permute-start.19 = (bf16[256,512]{1,0:T(8,128)(2,1)S(1)}, bf16[256,512]{1,0:T(8,128)(2,1)S(1)}, u32[]{:S(2)}, u32[]{:S(2)}) collective-permute-start(bf16[256,512]{1,0:T(8,128)(2,1)S(1)} %constant_dynamic-update-slice_fusion.4.refs_0_), channel_id=1, source_target_pairs={{0,8},{8,16},{16,24},{24,0},{1,9},{9,17},{17,25},{25,1},{2,10},{10... | collective-permute-start | bytes 786440 | tf_op jit(solution)/shard_map/ppermute | solution.py:255
  121.5 22.4 %collective-permute-start.39 = (bf16[256,512]{1,0:T(8,128)(2,1)S(1)}, bf16[256,512]{1,0:T(8,128)(2,1)S(1)}, u32[]{:S(2)}, u32[]{:S(2)}) collective-permute-start(bf16[256,512]{1,0:T(8,128)(2,1)S(1)} %constant_dynamic-update-slice_fusion.8.refs_0_), channel_id=1, source_target_pairs={{0,24},{8,0},{16,8},{24,16},{1,25},{9,1},{17,9},{25,17},{2,26},{10... | collective-permute-start | bytes 786440 | tf_op jit(solution)/shard_map/ppermute | solution.py:255
  124.7 19.2 %collective-permute-start.38 = (bf16[256,512]{1,0:T(8,128)(2,1)S(1)}, bf16[256,512]{1,0:T(8,128)(2,1)S(1)}, u32[]{:S(2)}, u32[]{:S(2)}) collective-permute-start(bf16[256,512]{1,0:T(8,128)(2,1)S(1)} %constant_dynamic-update-slice_fusion.8.refs_0_), channel_id=1, source_target_pairs={{0,16},{8,24},{16,0},{24,8},{1,17},{9,25},{17,1},{25,9},{2,18},{10... | collective-permute-start | bytes 786440 | tf_op jit(solution)/shard_map/ppermute | solution.py:255
  132.2 18.7 %collective-permute-start.37 = (bf16[256,512]{1,0:T(8,128)(2,1)S(1)}, bf16[256,512]{1,0:T(8,128)(2,1)S(1)}, u32[]{:S(2)}, u32[]{:S(2)}) collective-permute-start(bf16[256,512]{1,0:T(8,128)(2,1)S(1)} %constant_dynamic-update-slice_fusion.8.refs_0_), channel_id=1, source_target_pairs={{0,8},{8,16},{16,24},{24,0},{1,9},{9,17},{17,25},{25,1},{2,10},{10... | collective-permute-start | bytes 786440 | tf_op jit(solution)/shard_map/ppermute | solution.py:255
  142.2 9.7 %collective-permute-start.40 = (bf16[256,512]{1,0:T(8,128)(2,1)S(1)}, bf16[256,512]{1,0:T(8,128)(2,1)S(1)}, u32[]{:S(2)}, u32[]{:S(2)}) collective-permute-start(bf16[256,512]{1,0:T(8,128)(2,1)S(1)} %constant_dynamic-update-slice_fusion.8.refs_0_), channel_id=1, source_target_pairs={{0,4},{4,0},{1,5},{5,1},{2,6},{6,2},{3,7},{7,3},{8,12},{12,8},{9,1... | collective-permute-start | bytes 786440 | tf_op jit(solution)/shard_map/ppermute | solution.py:255
  151.8 12.6 %collective-permute-start.22 = (bf16[256,512]{1,0:T(8,128)(2,1)S(1)}, bf16[256,512]{1,0:T(8,128)(2,1)S(1)}, u32[]{:S(2)}, u32[]{:S(2)}) collective-permute-start(bf16[256,512]{1,0:T(8,128)(2,1)S(1)} %constant_dynamic-update-slice_fusion.4.refs_0_), channel_id=1, source_target_pairs={{0,4},{4,0},{1,5},{5,1},{2,6},{6,2},{3,7},{7,3},{8,12},{12,8},{9,1... | collective-permute-start | bytes 786440 | tf_op jit(solution)/shard_map/ppermute | solution.py:255
  151.8 13.7 %collective-permute-start.25 = (bf16[256,512]{1,0:T(8,128)(2,1)S(1)}, bf16[256,512]{1,0:T(8,128)(2,1)S(1)}, u32[]{:S(2)}, u32[]{:S(2)}) collective-permute-start(bf16[256,512]{1,0:T(8,128)(2,1)S(1)} %collective-permute-done.21.refs_3_), channel_id=1, source_target_pairs={{0,4},{4,0},{1,5},{5,1},{2,6},{6,2},{3,7},{7,3},{8,12},{12,8},{9,1... | collective-permute-start | bytes 786440 | tf_op jit(solution)/shard_map/ppermute | solution.py:255
  152.3 14.1 %collective-permute-start.24 = (bf16[256,512]{1,0:T(8,128)(2,1)S(1)}, bf16[256,512]{1,0:T(8,128)(2,1)S(1)}, u32[]{:S(2)}, u32[]{:S(2)}) collective-permute-start(bf16[256,512]{1,0:T(8,128)(2,1)S(1)} %collective-permute-done.20.refs_2_), channel_id=1, source_target_pairs={{0,4},{4,0},{1,5},{5,1},{2,6},{6,2},{3,7},{7,3},{8,12},{12,8},{9,1... | collective-permute-start | bytes 786440 | tf_op jit(solution)/shard_map/ppermute | solution.py:255
  153.0 13.5 %collective-permute-start.23 = (bf16[256,512]{1,0:T(8,128)(2,1)S(1)}, bf16[256,512]{1,0:T(8,128)(2,1)S(1)}, u32[]{:S(2)}, u32[]{:S(2)}) collective-permute-start(bf16[256,512]{1,0:T(8,128)(2,1)S(1)} %collective-permute-done.19.refs_1_), channel_id=1, source_target_pairs={{0,4},{4,0},{1,5},{5,1},{2,6},{6,2},{3,7},{7,3},{8,12},{12,8},{9,1... | collective-permute-start | bytes 786440 | tf_op jit(solution)/shard_map/ppermute | solution.py:255
  164.3 84.2 %collective-permute-start.14 = (bf16[256,640]{1,0:T(8,128)(2,1)S(1)}, bf16[256,640]{1,0:T(8,128)(2,1)S(1)}, u32[]{:S(2)}, u32[]{:S(2)}) collective-permute-start(bf16[256,640]{1,0:T(8,128)(2,1)S(1)} %normed_grad.1.n0), channel_id=1, source_target_pairs={{0,3},{1,0},{2,1},{3,2},{4,7},{5,4},{6,5},{7,6},{8,11},{9,8},{10,9... | collective-permute-start | bytes 983048 | tf_op jit(solution)/shard_map/ppermute | solution.py:255
  164.4 84.1 %collective-permute-start.13 = (bf16[256,640]{1,0:T(8,128)(2,1)S(1)}, bf16[256,640]{1,0:T(8,128)(2,1)}, u32[]{:S(2)}, u32[]{:S(2)}) collective-permute-start(bf16[256,640]{1,0:T(8,128)(2,1)S(1)} %normed_grad.1.n0), channel_id=1, source_target_pairs={{0,2},{1,3},{2,0},{3,1},{4,6},{5,7},{6,4},{7,5},{8,10},{9,11},{10,... | collective-permute-start | bytes 983048 | tf_op jit(solution)/shard_map/ppermute | solution.py:255
  165.6 83.0 %collective-permute-start.12 = (bf16[256,640]{1,0:T(8,128)(2,1)S(1)}, bf16[256,640]{1,0:T(8,128)(2,1)}, u32[]{:S(2)}, u32[]{:S(2)}) collective-permute-start(bf16[256,640]{1,0:T(8,128)(2,1)S(1)} %normed_grad.1.n0), channel_id=1, source_target_pairs={{0,1},{1,2},{2,3},{3,0},{4,5},{5,6},{6,7},{7,4},{8,9},{9,10},{10,1... | collective-permute-start | bytes 983048 | tf_op jit(solution)/shard_map/ppermute | solution.py:255
  (25 other events, 336.0 us)
